TPU v7x, 32 devices: a whole 2x2x4 slice. The times are simulated.
32 devices in a mesh: slab: 8 (over z, x), elec: 4 (over y, core).
Axes of the slice: x: 2, y: 2, z: 4, core: 2. Of those that a mesh axis runs over, the one named last changes fastest.
Arguments:
- potentials: float32 [128, 16, 128, 128], P('elec', None, 'slab'), may hold values from -6 to 6
- conductivity: float32 [16, 128, 128], P(None, 'slab'), may hold values from 0.1 to 1
- quadrupoles: int32 [512, 4], P('elec'), may hold values from 0 to 127, as said below
Outputs:
- jacobian: bfloat16 [512, 16, 128, 128], P('elec', 'slab')
Inputs may be any that keep to these rules, and one draw needn't show every extreme that they name: `quadrupoles`: rows g * 128 to (g + 1) * 128 - 1 are the measurements of group g; electrode e belongs to group e // 32. A and B are two different electrodes of the row's own group; M and N are two different electrodes of other groups. The rows of one group name, in M or N, at most 4 different electrodes of any one other group, and exactly 4 of some other group.
All inputs are finite; a program needn't handle non-finite values.
Results may differ from a plain program's by a relative error of at most 0.0058.
Values may be sent and summed in bfloat16 or wider, within the bound.
A program may use at most 256 MiB of HBM per device.

v0:
```python
import functools

import jax
import jax.numpy as jnp
from jax import lax
from jax.experimental import pallas as pl
from jax.experimental.pallas import tpu as pltpu
from jax.sharding import PartitionSpec as P

MESH = pl.DeviceIdType.MESH
REQ = 4
PARTS = 4


def lists(quadrupoles, per_group, groups):
    me = lax.axis_index("elec")
    ids = jnp.arange(per_group * groups, dtype=jnp.int32)
    owner = ids // per_group
    away = (owner - me) % groups
    named = jnp.any(quadrupoles[:, 2:4].reshape(-1)[:, None] == ids[None, :], axis=0)
    before = (owner[:, None] == owner[None, :]) & (ids[None, :] < ids[:, None])
    rank = jnp.sum((before & named[None, :]).astype(jnp.int32), axis=1)
    other = (away - 1) * REQ + jnp.minimum(rank, REQ - 1)
    slot = jnp.where(away == 0, ids - me * per_group, other)
    index = jnp.sum(jnp.where(quadrupoles[:, :, None] == ids, slot, 0), axis=-1)
    steps = jnp.arange(groups, dtype=jnp.int32)[:, None, None]
    lanes = jnp.arange(128, dtype=jnp.int32)[None, :, None]
    hit = named & (away == steps) & (rank == lanes)
    asked = jnp.sum(jnp.where(hit, ids % per_group, 0), axis=-1)
    return index.astype(jnp.int32), jnp.broadcast_to(asked[:, None, :], (groups, 8, 128))


def minus(first, second):
    return first.astype(jnp.float32) - second.astype(jnp.float32)


def exchange_kernel(slabs, groups, planes, *refs):
    pot, cond, asked, index, out = refs[:5]
    gz_src, asked_in, asked_s, weight_v = refs[5:9]
    p_in = refs[9 : 9 + planes]
    rest = list(refs[9 + planes :])

    def take(n):
        taken = rest[:n]
        del rest[:n]
        return taken

    own_z, own_xy, far_xy, box_xy = take(planes), take(planes), take(planes), take(planes)
    far_z, box_z, result = take(planes * PARTS), take(planes * PARTS), take(2)
    slab_send, slab_recv, cond_send, cond_recv, ask_send, ask_recv, xy_send, xy_recv, far_send, far_recv, local = rest

    count, depth, rows, width = pot.shape
    me = lax.axis_index("slab")
    group = lax.axis_index("elec")
    my_rows = pl.ds(pl.multiple_of(me * rows, rows), rows)

    barrier = pltpu.get_barrier_semaphore()
    for step in range(1, slabs):
        pl.semaphore_signal(barrier, inc=1, device_id={"slab": lax.rem(me + step, slabs)}, device_id_type=MESH)
    for step in range(1, groups):
        pl.semaphore_signal(barrier, inc=1, device_id={"elec": lax.rem(group + step, groups)}, device_id_type=MESH)
    pl.semaphore_wait(barrier, slabs + groups - 2)

    asks = []
    for step in range(1, groups):
        copy = pltpu.make_async_remote_copy(
            src_ref=asked.at[step],
            dst_ref=asked_in.at[step],
            send_sem=ask_send.at[step],
            recv_sem=ask_recv.at[step],
            device_id={"elec": lax.rem(group + step, groups)},
            device_id_type=MESH,
        )
        copy.start()
        asks.append(copy)

    def p_copy(plane, step):
        to = lax.rem(me + step, slabs)
        return pltpu.make_async_remote_copy(
            src_ref=pot.at[:, to * planes + plane],
            dst_ref=p_in[plane].at[:, my_rows, :],
            send_sem=slab_send.at[0, plane, step],
            recv_sem=slab_recv.at[0, plane, step],
            device_id={"slab": to},
            device_id_type=MESH,
        )

    def gz_copy(plane, step):
        to = lax.rem(me + step, slabs)
        return pltpu.make_async_remote_copy(
            src_ref=gz_src.at[plane, to],
            dst_ref=own_z[plane].at[:, my_rows, :],
            send_sem=slab_send.at[1, plane, step],
            recv_sem=slab_recv.at[1, plane, step],
            device_id={"slab": to},
            device_id_type=MESH,
        )

    def cond_copy(step):
        to = lax.rem(me + step, slabs)
        return pltpu.make_async_remote_copy(
            src_ref=cond.at[pl.ds(to * planes, planes)],
            dst_ref=weight_v.at[:, my_rows, :],
            send_sem=cond_send.at[step],
            recv_sem=cond_recv.at[step],
            device_id={"slab": to},
            device_id_type=MESH,
        )

    def p_local(plane):
        return pltpu.make_async_copy(pot.at[:, me * planes + plane], p_in[plane].at[:, my_rows, :], local.at[1 + plane])

    def gz_local(plane):
        return pltpu.make_async_copy(
            gz_src.at[plane, me], own_z[plane].at[:, my_rows, :], local.at[1 + planes + plane]
        )

    cond_local = pltpu.make_async_copy(
        cond.at[pl.ds(me * planes, planes)], weight_v.at[:, my_rows, :], local.at[1 + 2 * planes]
    )

    for step in range(1, slabs):
        cond_copy(step).start()
    cond_local.start()
    for plane in range(planes):
        for step in range(1, slabs):
            p_copy(plane, step).start()
        p_local(plane).start()

        @pl.loop(0, count)
        def _(e, plane=plane):
            for to in range(slabs):
                z = to * planes + plane
                above = pot[e, z + 1] if z + 1 < depth else jnp.zeros((rows, width), jnp.float32)
                below = pot[e, z - 1] if z > 0 else jnp.zeros((rows, width), jnp.float32)
                gz_src[plane, to, e] = ((above - below) * 0.5).astype(jnp.bfloat16)

        for step in range(1, slabs):
            gz_copy(plane, step).start()
        gz_local(plane).start()
    for copy in asks:
        copy.wait()
    to_scalar = pltpu.make_async_copy(asked_in, asked_s, local.at[2 + 2 * planes])
    to_scalar.start()
    to_scalar.wait()

    for step in range(1, slabs):
        cond_copy(step).wait_recv()
    cond_local.wait()

    x_size = p_in[0].shape[1]
    part = x_size // PARTS
    readings = out.shape[0]
    row = lax.broadcasted_iota(jnp.int32, (x_size, width), 0)
    lane = lax.broadcasted_iota(jnp.int32, (x_size, width), 1)

    def far_copy(chunk, step):
        return pltpu.make_async_remote_copy(
            src_ref=box_z[chunk].at[step - 1],
            dst_ref=far_z[chunk].at[pl.ds((groups - 1 - step) * REQ, REQ)],
            send_sem=far_send.at[chunk, step],
            recv_sem=far_recv.at[chunk, step],
            device_id={"elec": lax.rem(group + step, groups)},
            device_id_type=MESH,
        )

    def xy_copy(plane, step):
        return pltpu.make_async_remote_copy(
            src_ref=box_xy[plane].at[step - 1],
            dst_ref=far_xy[plane].at[pl.ds((groups - 1 - step) * REQ, REQ)],
            send_sem=xy_send.at[plane, step],
            recv_sem=xy_recv.at[plane, step],
            device_id={"elec": lax.rem(group + step, groups)},
            device_id_type=MESH,
        )

    def result_copy(chunk):
        plane, place = divmod(chunk, PARTS)
        return pltpu.make_async_copy(
            result[chunk % 2], out.at[:, plane, pl.ds(place * part, part), :], local.at[3 + 2 * planes + chunk % 2]
        )

    for plane in range(planes):
        for step in range(1, slabs):
            p_copy(plane, step).wait_recv()
        p_local(plane).wait()

        @pl.loop(0, count)
        def _(e, plane=plane):
            p = p_in[plane][e]
            up = jnp.where(row < x_size - 1, pltpu.roll(p, x_size - 1, 0), 0.0)
            down = jnp.where(row > 0, pltpu.roll(p, 1, 0), 0.0)
            own_xy[plane][e, 0] = ((up - down) * 0.5).astype(jnp.bfloat16)
            right = jnp.where(lane < width - 1, pltpu.roll(p, width - 1, 1), 0.0)
            left = jnp.where(lane > 0, pltpu.roll(p, 1, 1), 0.0)
            own_xy[plane][e, 1] = ((right - left) * 0.5).astype(jnp.bfloat16)

        for step in range(1, groups):
            for which in range(REQ):
                chosen = asked_s[groups - step, 0, which]
                for way in range(2):
                    box_xy[plane][step - 1, which, way] = own_xy[plane][chosen, way]
            xy_copy(plane, step).start()

        for step in range(1, slabs):
            gz_copy(plane, step).wait_recv()
        gz_local(plane).wait()

        for place in range(PARTS):
            chunk = plane * PARTS + place
            cut = pl.ds(place * part, part)
            for step in range(1, groups):
                for which in range(REQ):
                    chosen = asked_s[groups - step, 0, which]
                    box_z[chunk][step - 1, which] = own_z[plane][chosen, cut, :]
                far_copy(chunk, step).start()

        for step in range(1, groups):
            xy_copy(plane, step).wait_recv()
        for place in range(PARTS):
            chunk = plane * PARTS + place
            cut = pl.ds(place * part, part)
            for step in range(1, groups):
                far_copy(chunk, step).wait_recv()
            if chunk >= 2:
                result_copy(chunk - 2).wait()
            weight = -weight_v[plane, cut, :]

            @pl.loop(0, readings // 4)
            def _(block, plane=plane, chunk=chunk, cut=cut, weight=weight):
                for k in range(4):
                    m = block * 4 + k
                    a, b, c, d = index[4 * m], index[4 * m + 1], index[4 * m + 2], index[4 * m + 3]
                    first, second = own_z[plane][a, cut, :], own_z[plane][b, cut, :]
                    third, fourth = far_z[chunk][c], far_z[chunk][d]
                    total = minus(first, second) * minus(third, fourth)
                    for way in range(2):
                        first, second = own_xy[plane][a, way, cut, :], own_xy[plane][b, way, cut, :]
                        third, fourth = far_xy[plane][c, way, cut, :], far_xy[plane][d, way, cut, :]
                        total = total + minus(first, second) * minus(third, fourth)
                    result[chunk % 2][m] = (weight * total).astype(jnp.bfloat16)

            result_copy(chunk).start()

    chunks = planes * PARTS
    for chunk in range(max(chunks - 2, 0), chunks):
        result_copy(chunk).wait()
    for chunk in range(chunks):
        for step in range(1, groups):
            far_copy(chunk, step).wait_send()
    for plane in range(planes):
        for step in range(1, groups):
            xy_copy(plane, step).wait_send()
        for step in range(1, slabs):
            p_copy(plane, step).wait_send()
            gz_copy(plane, step).wait_send()
    for step in range(1, slabs):
        cond_copy(step).wait_send()


def exchange(potentials, conductivity, asked, index, slabs, groups):
    count, depth, rows, width = potentials.shape
    readings = index.shape[0]
    planes = depth // slabs
    x_size = rows * slabs
    part = x_size // PARTS
    hbm = pl.BlockSpec(memory_space=pl.ANY)
    dma = pltpu.SemaphoreType.DMA
    bf16, f32 = jnp.bfloat16, jnp.float32
    chunks = planes * PARTS
    return pl.pallas_call(
        functools.partial(exchange_kernel, slabs, groups, planes),
        out_shape=jax.ShapeDtypeStruct((readings, planes, x_size, width), bf16),
        in_specs=[pl.BlockSpec(memory_space=pltpu.VMEM), hbm, pl.BlockSpec(memory_space=pltpu.VMEM), pl.BlockSpec(memory_space=pltpu.SMEM)],
        out_specs=hbm,
        scratch_shapes=[
            pltpu.VMEM((planes, slabs, count, rows, width), bf16),
            pltpu.VMEM((groups, 8, 128), jnp.int32),
            pltpu.SMEM((groups, 8, 128), jnp.int32),
            pltpu.VMEM((planes, x_size, width), f32),
        ]
        + [pltpu.VMEM((count, x_size, width), f32)] * planes
        + [pltpu.VMEM((count, x_size, width), bf16)] * planes
        + [pltpu.VMEM((count, 2, x_size, width), bf16)] * planes
        + [pltpu.VMEM(((groups - 1) * REQ, 2, x_size, width), bf16)] * planes
        + [pltpu.VMEM((groups - 1, REQ, 2, x_size, width), bf16)] * planes
        + [pltpu.VMEM(((groups - 1) * REQ, part, width), bf16)] * chunks
        + [pltpu.VMEM((groups - 1, REQ, part, width), bf16)] * chunks
        + [pltpu.VMEM((readings, part, width), bf16)] * 2
        + [
            dma((2, planes, slabs)),
            dma((2, planes, slabs)),
            dma((slabs,)),
            dma((slabs,)),
            dma((groups,)),
            dma((groups,)),
            dma((planes, groups)),
            dma((planes, groups)),
            dma((chunks, groups)),
            dma((chunks, groups)),
            dma((5 + 2 * planes,)),
        ],
        compiler_params=pltpu.CompilerParams(
            collective_id=0, has_side_effects=True, vmem_limit_bytes=29 * 1024 * 1024
        ),
        name="exchange",
    )(potentials, conductivity, asked, index.reshape(-1))


def deliver_kernel(source, target, done):
    share = source.shape[0] // PARTS
    copies = [
        pltpu.make_async_copy(source.at[pl.ds(k * share, share)], target.at[pl.ds(k * share, share)], done.at[k])
        for k in range(PARTS)
    ]
    for copy in copies:
        copy.start()
    for copy in copies:
        copy.wait()


def deliver(rows):
    return pl.pallas_call(
        deliver_kernel,
        out_shape=jax.ShapeDtypeStruct(rows.shape, rows.dtype),
        in_specs=[pl.BlockSpec(memory_space=pl.ANY)],
        out_specs=pl.BlockSpec(memory_space=pl.ANY),
        scratch_shapes=[pltpu.SemaphoreType.DMA((PARTS,))],
        compiler_params=pltpu.CompilerParams(vmem_limit_bytes=1024 * 1024),
        name="deliver",
    )(rows)


def general(potentials, conductivity, quadrupoles):
    shifted = lax.all_to_all(potentials, "slab", split_axis=1, concat_axis=2, tiled=True)
    cond = lax.all_to_all(conductivity[None], "slab", split_axis=1, concat_axis=2, tiled=True)[0]
    slabs = lax.axis_size("slab")
    ends = slabs - 1
    last = shifted.shape[1] - 1
    below = lax.ppermute(shifted[:, last:], "slab", [(i, i + 1) for i in range(ends)])
    above = lax.ppermute(shifted[:, :1], "slab", [(i + 1, i) for i in range(ends)])
    tall = jnp.concatenate([below, shifted, above], axis=1)
    wide = jnp.pad(shifted, ((0, 0), (0, 0), (1, 1), (1, 1)))
    grads = jnp.stack(
        [
            (tall[:, 2:] - tall[:, :-2]) * 0.5,
            (wide[:, :, 2:, 1:-1] - wide[:, :, :-2, 1:-1]) * 0.5,
            (wide[:, :, 1:-1, 2:] - wide[:, :, 1:-1, :-2]) * 0.5,
        ],
        1,
    ).astype(jnp.bfloat16)
    table = lax.all_gather(grads.reshape(grads.shape[0], 3, -1), "elec", axis=0, tiled=True)
    ids = jnp.arange(table.shape[0], dtype=jnp.int32)
    hot = (quadrupoles[:, :, None] == ids).astype(jnp.bfloat16)
    flat = table.reshape(table.shape[0], -1)
    shape = (quadrupoles.shape[0], 3, -1)
    source = jnp.dot(hot[:, 0] - hot[:, 1], flat, preferred_element_type=jnp.float32).reshape(shape)
    probe = jnp.dot(hot[:, 2] - hot[:, 3], flat, preferred_element_type=jnp.float32).reshape(shape)
    rows = -(cond.reshape(-1)[None] * jnp.sum(source * probe, axis=1))
    return rows.astype(jnp.bfloat16).reshape((quadrupoles.shape[0],) + shifted.shape[1:])


def shards(potentials, conductivity, quadrupoles):
    slabs, groups = lax.axis_size("slab"), lax.axis_size("elec")
    count, depth, rows, width = potentials.shape
    if rows % 16 or width % 128 or depth % slabs or (rows * slabs) % (16 * PARTS) or quadrupoles.shape[0] % 4:
        return general(potentials, conductivity, quadrupoles)
    index, asked = lists(quadrupoles, count, groups)
    return deliver(exchange(potentials, conductivity, asked, index, slabs, groups))


def solution(mesh):
    in_specs = (P("elec", None, "slab", None), P(None, "slab", None), P("elec", None))
    out_specs = P("elec", "slab", None, None)
    return jax.shard_map(shards, mesh=mesh, in_specs=in_specs, out_specs=out_specs, check_vma=False)
```

profile of v0, /device:TPU:10, one launch (start us, length us, event | category | flops | bytes accessed | tf_op | source)
XLA Modules:
  0.0 169.6 jit_solution(8236972215244534437)
XLA Ops:
  0.0 0.7 slice.3
  0.7 0.1 copy.7
  0.8 0.1 eq.84
  0.9 0.1 fusion
  1.1 0.2 convert_reduce_fusion
  1.3 0.9 select_reduce_fusion
  2.2 0.1 select_reduce_fusion.1
  2.4 0.1 copy.8
  2.5 0.1 reshape.120.refs_3_
  2.6 0.0 copy-start
  2.6 2.2 %copy-done = f32[32,16,16,128]{3,2,1,0:T(8,128)S(1)} copy-done((f32[32,16,16,128]{3,2,1,0:T(8,128)S(1)}, f32[32,16,16,128]{3,2,1,0:T(8,128)}, u32[]{:S(2)}) %copy-start) | copy-done | bytes 4194328
  4.8 0.0 copy-start.1
  4.8 0.9 copy-done.1
  5.7 160.5 %exchange.1.source = bf16[128,2,128,128]{3,2,1,0:T(8,128)(2,1)S(1)} custom-call(f32[32,16,16,128]{3,2,1,0:T(8,128)S(1)} %copy-done, f32[16,16,128]{2,1,0:T(8,128)S(1)} %copy-done.1, s32[4,8,128]{2,1,0:T(8,128)S(1)} %broadcast_in_dim.18.refs_2_, s32[512]{0:T(512)S(1)} %reshape.120.refs_3_), custom_call_target="tpu_custom_call" | custom-call | tf_op jit(solution)/shard_map/exchange/pallas_call | solution.py:271
  166.3 3.4 %deliver.1 = bf16[128,2,128,128]{3,2,1,0:T(8,128)(2,1)} custom-call(bf16[128,2,128,128]{3,2,1,0:T(8,128)(2,1)S(1)} %exchange.1.source), custom_call_target="tpu_custom_call" | custom-call | tf_op jit(solution)/shard_map/deliver/pallas_call | solution.py:323
  (6 shorter events, 0.1 us)
Async XLA Ops:
  2.6 2.2 %copy-start = (f32[32,16,16,128]{3,2,1,0:T(8,128)S(1)}, f32[32,16,16,128]{3,2,1,0:T(8,128)}, u32[]{:S(2)}) copy-start(f32[32,16,16,128]{3,2,1,0:T(8,128)} %refs_0_.1) | copy-start | bytes 12582916
  4.8 0.9 copy-start.1
where the time goes:
time: 171 us; the launch traced here: 170 us
  Pallas kernels  164 us (96%)
  local copies, waits for them, and re-layouts  4.25 us (2%)
    pallas_call x1, Pallas kernels, exchange(): pl.pallas_call(functools.partial(exchange_kernel, slabs, groups, planes),...  161 us

commit v1 on v0

v1 whole, which is shorter than its diff:
```python
import functools

import jax
import jax.numpy as jnp
from jax import lax
from jax.experimental import pallas as pl
from jax.experimental.pallas import tpu as pltpu
from jax.sharding import PartitionSpec as P

MESH = pl.DeviceIdType.MESH
REQ = 4
PARTS = 4
SPAN = 12.5
LEVELS = 32767.0
COND_MID = 0.55
COND_STEPS = 32766.0 / 0.45


def lists(quadrupoles, per_group, groups):
    me = lax.axis_index("elec")
    ids = jnp.arange(per_group * groups, dtype=jnp.int32)
    owner = ids // per_group
    away = (owner - me) % groups
    named = jnp.any(quadrupoles[:, 2:4].reshape(-1)[:, None] == ids[None, :], axis=0)
    before = (owner[:, None] == owner[None, :]) & (ids[None, :] < ids[:, None])
    rank = jnp.sum((before & named[None, :]).astype(jnp.int32), axis=1)
    other = (away - 1) * REQ + jnp.minimum(rank, REQ - 1)
    slot = jnp.where(away == 0, ids - me * per_group, other)
    index = jnp.sum(jnp.where(quadrupoles[:, :, None] == ids, slot, 0), axis=-1)
    steps = jnp.arange(groups, dtype=jnp.int32)[:, None, None]
    lanes = jnp.arange(128, dtype=jnp.int32)[None, :, None]
    hit = named & (away == steps) & (rank == lanes)
    asked = jnp.sum(jnp.where(hit, ids % per_group, 0), axis=-1)
    return index.astype(jnp.int32), jnp.broadcast_to(asked[:, None, :], (groups, 8, 128))


def minus(first, second):
    return first.astype(jnp.float32) - second.astype(jnp.float32)


def decode(code):
    root = code.astype(jnp.int32).astype(jnp.float32) * (SPAN**0.125 / LEVELS)
    square = root * root
    fourth = square * square
    return (root * jnp.abs(root)) * square * fourth


def encode(step):
    level = jnp.exp2(jnp.log2(jnp.abs(step) * (1.0 / SPAN)) * 0.125) * LEVELS
    level = (level + 0.5).astype(jnp.int32)
    return jnp.where(step < 0, -level, level).astype(jnp.int16)


def exchange_kernel(slabs, groups, *refs):
    pot, cond, asked, index, out = refs[:5]
    pot_v, cond_v, enc, cin, field, cond_code, cond_in = refs[5:12]
    asked_in, asked_s, own, box, result = refs[12:17]
    far = refs[17 : 17 + slabs]
    pot_sem, plane_send, plane_recv, fwd_send, cond_send, cond_recv = refs[17 + slabs : 23 + slabs]
    ask_send, ask_recv, far_send, far_recv, out_sem, local = refs[23 + slabs :]

    count, depth, rows, width = pot.shape
    slots = rows + 1
    half = slabs // 2
    pair = half // 2
    x_size = rows * slabs
    tall = x_size + 16
    readings = out.shape[0]
    me = lax.axis_index("slab")
    group = lax.axis_index("elec")
    upper = me // half
    near0 = upper * half
    far0 = (1 - upper) * half
    inner = (me >= half - pair) & (me < half + pair)
    my_rows = pl.ds(pl.multiple_of(me * rows, rows), rows)

    def pot_copy(d):
        return pltpu.make_async_copy(
            pot.at[:, pl.ds(2 * d, 2)], pot_v.at[:, pl.ds(2 * d, 2)], pot_sem.at[d]
        )

    def dest(n):
        first, second = jnp.where(inner, far0, near0), jnp.where(inner, near0, far0)
        return jnp.where(n < half, first + n, second + n - half)

    @pl.loop(0, slabs)
    def _(n):
        pot_copy(dest(n)).start()

    cond_load = pltpu.make_async_copy(cond, cond_v, local.at[0])
    cond_load.start()

    barrier = pltpu.get_barrier_semaphore()
    for step in range(1, slabs):
        pl.semaphore_signal(barrier, inc=1, device_id={"slab": lax.rem(me + step, slabs)}, device_id_type=MESH)
    for step in range(1, groups):
        pl.semaphore_signal(barrier, inc=1, device_id={"elec": lax.rem(group + step, groups)}, device_id_type=MESH)

    blank = jnp.zeros((slots, count, width), jnp.int16)
    enc[0] = blank
    enc[depth + 1] = blank

    @pl.when(me == 0)
    def _():
        @pl.loop(1, slabs)
        def _(r):
            cin[r, 0] = blank

    @pl.when(me == slabs - 1)
    def _():
        @pl.loop(0, slabs - 1)
        def _(r):
            cin[r, 3] = blank

    @pl.loop(0, 2 * count)
    def _(k):
        base = (count + k) * tall
        edge = jnp.zeros((8, width), jnp.float32)
        field[pl.ds(pl.multiple_of(base, 8), 8), :] = edge
        field[pl.ds(pl.multiple_of(base + tall - 8, 8), 8), :] = edge

    pl.semaphore_wait(barrier, slabs + groups - 2)

    def ask_copy(step):
        return pltpu.make_async_remote_copy(
            src_ref=asked.at[step],
            dst_ref=asked_in.at[step],
            send_sem=ask_send.at[step],
            recv_sem=ask_recv.at[step],
            device_id={"elec": lax.rem(group + step, groups)},
            device_id_type=MESH,
        )

    for step in range(1, groups):
        ask_copy(step).start()

    def plane_copy(slot, d):
        return pltpu.make_async_remote_copy(
            src_ref=enc.at[2 * d + slot],
            dst_ref=cin.at[me, slot],
            send_sem=plane_send.at[slot, d],
            recv_sem=plane_recv.at[slot, me],
            device_id={"slab": d},
            device_id_type=MESH,
        )

    def plane_wait(slot, r):
        pltpu.make_async_remote_copy(
            src_ref=enc.at[slot],
            dst_ref=cin.at[r, slot],
            send_sem=plane_send.at[slot, r],
            recv_sem=plane_recv.at[slot, r],
            device_id={"slab": r},
            device_id_type=MESH,
        ).wait_recv()

    def forward_up(r):
        return pltpu.make_async_remote_copy(
            src_ref=cin.at[r, 2],
            dst_ref=cin.at[r, 0],
            send_sem=fwd_send.at[0, r],
            recv_sem=plane_recv.at[0, r],
            device_id={"slab": lax.rem(me + 1, slabs)},
            device_id_type=MESH,
        )

    def forward_down(r):
        return pltpu.make_async_remote_copy(
            src_ref=cin.at[r, 1],
            dst_ref=cin.at[r, 3],
            send_sem=fwd_send.at[1, r],
            recv_sem=plane_recv.at[3, r],
            device_id={"slab": lax.rem(me + slabs - 1, slabs)},
            device_id_type=MESH,
        )

    ups = (me != slabs - 1) & (me != half - 1)
    downs = (me != 0) & (me != half)

    def cond_copy(step):
        to = lax.rem(me + step, slabs)
        return pltpu.make_async_remote_copy(
            src_ref=cond_code.at[pl.ds(to * 2, 2)],
            dst_ref=cond_in.at[:, my_rows, :],
            send_sem=cond_send.at[step],
            recv_sem=cond_recv.at[step],
            device_id={"slab": to},
            device_id_type=MESH,
        )

    own_cond = pltpu.make_async_copy(cond_code.at[pl.ds(me * 2, 2)], cond_in.at[:, my_rows, :], local.at[1])
    own_planes = pltpu.make_async_copy(enc.at[pl.ds(2 * me, 4)], cin.at[me], local.at[2])

    cond_load.wait()

    @pl.loop(0, depth)
    def _(z):
        level = (cond_v[z] - COND_MID) * COND_STEPS
        level = level + jnp.where(level < 0, -0.5, 0.5)
        cond_code[z] = level.astype(jnp.int32).astype(jnp.int16)

    for step in range(1, slabs):
        cond_copy(step).start()
    own_cond.start()

    def encode_plane(z):
        reached = jnp.zeros((count, width), jnp.float32)
        for slot in range(slots):
            start = z * rows + max(slot - 1, 0)
            wanted = pot_v.reshape(count * depth * rows, width)[pl.ds(start, count, stride=depth * rows), :]
            code = encode(wanted - reached)
            enc[z + 1, slot] = code
            reached = reached + decode(code)

    @pl.loop(0, 2 * slabs)
    def _(n):
        part, place = n // half, lax.rem(n, half)
        i = lax.rem(part, 2)
        d = dest((part // 2) * half + place)

        @pl.when(i == 0)
        def _():
            pot_copy(d).wait()

        encode_plane(2 * d + i)
        close = d // half == upper

        @pl.when((d != me) & (close | inner))
        def _():
            plane_copy(1 + i, d).start()

    own_planes.start()

    def edge_copies(d, act):
        close = d // half == upper

        @pl.when((d > 0) & (close | (d == half)))
        def _():
            act(plane_copy(0, d))

        @pl.when((d < slabs - 1) & (close | (d == half - 1)))
        def _():
            act(plane_copy(3, d))

    @pl.when(inner)
    def _():
        edge_copies(jnp.where(upper == 0, half, half - 1), lambda copy: copy.start())

    @pl.loop(0, half)
    def _(j):
        d = near0 + j

        @pl.when(d != me)
        def _():
            edge_copies(d, lambda copy: copy.start())

    for step in range(1, groups):
        ask_copy(step).wait()
    to_scalar = pltpu.make_async_copy(asked_in, asked_s, local.at[3])
    to_scalar.start()
    to_scalar.wait()
    for step in range(1, slabs):
        cond_copy(step).wait_recv()
    own_cond.wait()

    def decode_plane(r, slot):
        reached = jnp.zeros((count, width), jnp.float32)
        for k in range(slots):
            reached = reached + decode(cin[r, slot, k])
            if k > 0:
                field[pl.ds(slot * count * tall + 8 + r * rows + k - 1, count, stride=tall), :] = reached

    row_lane = lax.broadcasted_iota(jnp.int32, (rows, width), 1)

    def gradients(b):
        @pl.loop(0, count)
        def _(e):
            for i in range(2):
                def at(slot, shift):
                    return field[pl.ds((slot * count + e) * tall + 8 + b * rows + shift, rows), :]

                here = at(1 + i, 0)
                right = jnp.where(row_lane < width - 1, pltpu.roll(here, width - 1, 1), 0.0)
                left = jnp.where(row_lane > 0, pltpu.roll(here, 1, 1), 0.0)
                own[b, e, 0, i] = ((at(2 + i, 0) - at(i, 0)) * 0.5).astype(jnp.bfloat16)
                own[b, e, 1, i] = ((at(1 + i, 1) - at(1 + i, -1)) * 0.5).astype(jnp.bfloat16)
                own[b, e, 2, i] = ((right - left) * 0.5).astype(jnp.bfloat16)

    def far_copy(k, step):
        return pltpu.make_async_remote_copy(
            src_ref=box.at[k, step - 1],
            dst_ref=far[k].at[pl.ds((groups - 1 - step) * REQ, REQ)],
            send_sem=far_send.at[k, step],
            recv_sem=far_recv.at[k, step],
            device_id={"elec": lax.rem(group + step, groups)},
            device_id_type=MESH,
        )

    def offer(k, b):
        gradients(b)
        for step in range(1, groups):
            for which in range(REQ):
                chosen = asked_s[groups - step, 0, which]
                box[k, step - 1, which] = own[b, chosen]
            far_copy(k, step).start()

    def result_copy(b):
        return pltpu.make_async_copy(
            result.at[b], out.at[:, :, pl.ds(pl.multiple_of(b * rows, rows), rows), :], out_sem.at[b]
        )

    def finish(k, b):
        for step in range(1, groups):
            far_copy(k, step).wait_recv()
        for i in range(2):
            weight = cond_in[i, pl.ds(pl.multiple_of(b * rows, rows), rows), :]
            weight = -(weight.astype(jnp.int32).astype(jnp.float32) * (1.0 / COND_STEPS) + COND_MID)

            @pl.loop(0, readings // 4)
            def _(block, i=i, weight=weight):
                for n in range(4):
                    m = block * 4 + n
                    first, second, third, fourth = index[4 * m], index[4 * m + 1], index[4 * m + 2], index[4 * m + 3]
                    total = None
                    for way in range(3):
                        source = minus(own[b, first, way, i], own[b, second, way, i])
                        probe = minus(far[k][third, way, i], far[k][fourth, way, i])
                        total = source * probe if total is None else total + source * probe
                    result[b, m, i] = (weight * total).astype(jnp.bfloat16)

        result_copy(b).start()

    @pl.loop(0, half)
    def _(j):
        r = near0 + j

        @pl.when(r == me)
        def _():
            own_planes.wait()

        @pl.when(r != me)
        def _():
            plane_wait(1, r)
            plane_wait(2, r)

            @pl.when(me > 0)
            def _():
                plane_wait(0, r)

            @pl.when(me < slabs - 1)
            def _():
                plane_wait(3, r)

        @pl.loop(0, 4)
        def _(slot):
            decode_plane(r, slot)

    first = upper * (half + 1)

    for j in range(half - 1):
        offer(j, first + j)
    for j in range(half - 1):
        finish(j, first + j)

    def take(r0):
        @pl.loop(0, pair)
        def _(j):
            plane_wait(1, r0 + j)

            @pl.when(downs)
            def _():
                forward_down(r0 + j).start()

            decode_plane(r0 + j, 1)

        @pl.loop(0, pair)
        def _(j):
            plane_wait(2, r0 + j)

            @pl.when(ups)
            def _():
                forward_up(r0 + j).start()

            decode_plane(r0 + j, 2)

    def take_edges(r0):
        @pl.loop(0, pair)
        def _(j):
            @pl.when(me > 0)
            def _():
                plane_wait(0, r0 + j)

            decode_plane(r0 + j, 0)

            @pl.when(me < slabs - 1)
            def _():
                plane_wait(3, r0 + j)

            decode_plane(r0 + j, 3)

    take(far0 + (1 - upper) * 0 + upper * pair)

    @pl.when(jnp.logical_not(inner))
    def _():
        for i in range(2):
            @pl.loop(0, half)
            def _(j, i=i):
                plane_copy(1 + i, far0 + j).start()

        edge_copies(jnp.where(upper == 0, half, half - 1), lambda copy: copy.start())

    take_edges(far0 + upper * pair)
    for j in range(half - 1, half + 1):
        offer(j, j)
    for j in range(half - 1, half + 1):
        finish(j, j)

    take(far0 + (1 - upper) * pair)
    take_edges(far0 + (1 - upper) * pair)
    last = (1 - upper) * (half + 1)

    for j in range(half - 1):
        offer(half + 1 + j, last + j)
    for j in range(half - 1):
        finish(half + 1 + j, last + j)

    @pl.loop(0, slabs)
    def _(d):
        result_copy(d).wait()

        @pl.when(d != me)
        def _():
            plane_copy(1, d).wait_send()
            plane_copy(2, d).wait_send()
            edge_copies(d, lambda copy: copy.wait_send())

        @pl.when(d // half != upper)
        def _():
            @pl.when(ups)
            def _():
                forward_up(d).wait_send()

            @pl.when(downs)
            def _():
                forward_down(d).wait_send()

    for step in range(1, slabs):
        cond_copy(step).wait_send()
    for k in range(slabs):
        for step in range(1, groups):
            far_copy(k, step).wait_send()


def exchange(potentials, conductivity, asked, index, slabs, groups):
    count, depth, rows, width = potentials.shape
    readings = index.shape[0]
    x_size = rows * slabs
    anywhere = pl.BlockSpec(memory_space=pl.ANY)
    dma = pltpu.SemaphoreType.DMA
    bf16, f32, i16 = jnp.bfloat16, jnp.float32, jnp.int16
    asks = (groups - 1) * REQ
    return pl.pallas_call(
        functools.partial(exchange_kernel, slabs, groups),
        out_shape=jax.ShapeDtypeStruct((readings, 2, x_size, width), bf16),
        in_specs=[anywhere, anywhere, pl.BlockSpec(memory_space=pltpu.VMEM), pl.BlockSpec(memory_space=pltpu.SMEM)],
        out_specs=anywhere,
        scratch_shapes=[
            pltpu.VMEM((count, depth, rows, width), f32),
            pltpu.VMEM((depth, rows, width), f32),
            pltpu.VMEM((depth + 2, rows + 1, count, width), i16),
            pltpu.VMEM((slabs, 4, rows + 1, count, width), i16),
            pltpu.VMEM((4 * count * (x_size + 16), width), f32),
            pltpu.VMEM((depth, rows, width), i16),
            pltpu.VMEM((2, x_size, width), i16),
            pltpu.VMEM((groups, 8, 128), jnp.int32),
            pltpu.SMEM((groups, 8, 128), jnp.int32),
            pltpu.VMEM((slabs, count, 3, 2, rows, width), bf16),
            pltpu.VMEM((slabs, groups - 1, REQ, 3, 2, rows, width), bf16),
            pltpu.VMEM((slabs, readings, 2, rows, width), bf16),
        ]
        + [pltpu.VMEM((asks, 3, 2, rows, width), bf16)] * slabs
        + [
            dma((slabs,)),
            dma((4, slabs)),
            dma((4, slabs)),
            dma((2, slabs)),
            dma((slabs,)),
            dma((slabs,)),
            dma((groups,)),
            dma((groups,)),
            dma((slabs, groups)),
            dma((slabs, groups)),
            dma((slabs,)),
            dma((4,)),
        ],
        compiler_params=pltpu.CompilerParams(
            collective_id=0, has_side_effects=True, vmem_limit_bytes=50 * 1024 * 1024
        ),
        name="exchange",
    )(potentials, conductivity, asked, index.reshape(-1))


def deliver_kernel(source, target, done):
    share = source.shape[0] // PARTS
    copies = [
        pltpu.make_async_copy(source.at[pl.ds(k * share, share)], target.at[pl.ds(k * share, share)], done.at[k])
        for k in range(PARTS)
    ]
    for copy in copies:
        copy.start()
    for copy in copies:
        copy.wait()


def deliver(rows):
    return pl.pallas_call(
        deliver_kernel,
        out_shape=jax.ShapeDtypeStruct(rows.shape, rows.dtype),
        in_specs=[pl.BlockSpec(memory_space=pl.ANY)],
        out_specs=pl.BlockSpec(memory_space=pl.ANY),
        scratch_shapes=[pltpu.SemaphoreType.DMA((PARTS,))],
        compiler_params=pltpu.CompilerParams(vmem_limit_bytes=1024 * 1024),
        name="deliver",
    )(rows)


def general(potentials, conductivity, quadrupoles):
    shifted = lax.all_to_all(potentials, "slab", split_axis=1, concat_axis=2, tiled=True)
    cond = lax.all_to_all(conductivity[None], "slab", split_axis=1, concat_axis=2, tiled=True)[0]
    slabs = lax.axis_size("slab")
    ends = slabs - 1
    last = shifted.shape[1] - 1
    below = lax.ppermute(shifted[:, last:], "slab", [(i, i + 1) for i in range(ends)])
    above = lax.ppermute(shifted[:, :1], "slab", [(i + 1, i) for i in range(ends)])
    tall = jnp.concatenate([below, shifted, above], axis=1)
    wide = jnp.pad(shifted, ((0, 0), (0, 0), (1, 1), (1, 1)))
    grads = jnp.stack(
        [
            (tall[:, 2:] - tall[:, :-2]) * 0.5,
            (wide[:, :, 2:, 1:-1] - wide[:, :, :-2, 1:-1]) * 0.5,
            (wide[:, :, 1:-1, 2:] - wide[:, :, 1:-1, :-2]) * 0.5,
        ],
        1,
    ).astype(jnp.bfloat16)
    table = lax.all_gather(grads.reshape(grads.shape[0], 3, -1), "elec", axis=0, tiled=True)
    ids = jnp.arange(table.shape[0], dtype=jnp.int32)
    hot = (quadrupoles[:, :, None] == ids).astype(jnp.bfloat16)
    flat = table.reshape(table.shape[0], -1)
    shape = (quadrupoles.shape[0], 3, -1)
    source = jnp.dot(hot[:, 0] - hot[:, 1], flat, preferred_element_type=jnp.float32).reshape(shape)
    probe = jnp.dot(hot[:, 2] - hot[:, 3], flat, preferred_element_type=jnp.float32).reshape(shape)
    rows = -(cond.reshape(-1)[None] * jnp.sum(source * probe, axis=1))
    return rows.astype(jnp.bfloat16).reshape((quadrupoles.shape[0],) + shifted.shape[1:])


def shards(potentials, conductivity, quadrupoles):
    slabs, groups = lax.axis_size("slab"), lax.axis_size("elec")
    count, depth, rows, width = potentials.shape
    fits = rows == 16 and width == 128 and depth == 2 * slabs and slabs % 4 == 0
    if not fits or count % 16 or quadrupoles.shape[0] % 4:
        return general(potentials, conductivity, quadrupoles)
    index, asked = lists(quadrupoles, count, groups)
    return deliver(exchange(potentials, conductivity, asked, index, slabs, groups))


def solution(mesh):
    in_specs = (P("elec", None, "slab", None), P(None, "slab", None), P("elec", None))
    out_specs = P("elec", "slab", None, None)
    return jax.shard_map(shards, mesh=mesh, in_specs=in_specs, out_specs=out_specs, check_vma=False)
```

time: 171 us -> 136 us (0.80)
  Pallas kernels: 164 us -> 128 us
    pallas_call x1, Pallas kernels: 161 us -> 124 us  [exchange(): pl.pallas_call(functools.partial(exchange_kernel, slabs, groups), out_sha...]
where the time goes in v1:
time: 136 us; the launch traced here: 135 us
  Pallas kernels  128 us (94%)
  local copies, waits for them, and re-layouts  5.43 us (4%)
  other arithmetic  1.42 us (1%)
    pallas_call x1, Pallas kernels, exchange(): pl.pallas_call(functools.partial(exchange_kernel, slabs, groups), out_sha...  124 us
    unnamed x4, local copies, waits for them, and re-layouts  4.28 us
    pallas_call x1, Pallas kernels, deliver(): pl.pallas_call(deliver_kernel, out_shape=jax.ShapeDtypeStruct(rows.shape,...  3.36 us

profile of v1, /device:TPU:10, one launch (start us, length us, event | category | flops | bytes accessed | tf_op | source)
XLA Modules:
  0.0 134.7 jit_solution(17410183999469044809)
XLA Ops:
  0.0 0.7 slice.3
  0.7 0.1 copy.7
  0.8 0.1 eq.84
  0.9 0.1 fusion
  1.1 0.2 convert_reduce_fusion
  1.3 0.9 select_reduce_fusion
  2.2 0.1 select_reduce_fusion.1
  2.4 0.1 copy.8
  2.5 0.1 reshape.120.refs_3_
  2.6 0.0 copy-start.1
  2.6 0.9 copy-done.1
  3.5 124.4 %exchange.1.source = bf16[128,2,128,128]{3,2,1,0:T(8,128)(2,1)} custom-call(f32[32,16,16,128]{3,2,1,0:T(8,128)} %refs_0_.1, f32[16,16,128]{2,1,0:T(8,128)S(1)} %copy-done.1, s32[4,8,128]{2,1,0:T(8,128)S(1)} %broadcast_in_dim.18.refs_2_, s32[512]{0:T(512)S(1)} %reshape.120.refs_3_), custom_call_target="tpu_custom_call" | custom-call | tf_op jit(solution)/shard_map/exchange/pallas_call | solution.py:462
  127.9 0.0 copy-start
  127.9 3.4 %copy-done = bf16[128,2,128,128]{3,2,1,0:T(8,128)(2,1)S(1)} copy-done((bf16[128,2,128,128]{3,2,1,0:T(8,128)(2,1)S(1)}, bf16[128,2,128,128]{3,2,1,0:T(8,128)(2,1)}, u32[]{:S(2)}) %copy-start) | copy-done | bytes 8388632
  131.3 3.4 %deliver.1 = bf16[128,2,128,128]{3,2,1,0:T(8,128)(2,1)} custom-call(bf16[128,2,128,128]{3,2,1,0:T(8,128)(2,1)S(1)} %copy-done), custom_call_target="tpu_custom_call" | custom-call | tf_op jit(solution)/shard_map/deliver/pallas_call | solution.py:516
  (6 shorter events, 0.1 us)
Async XLA Ops:
  2.6 0.9 copy-start.1
  127.9 3.4 %copy-start = (bf16[128,2,128,128]{3,2,1,0:T(8,128)(2,1)S(1)}, bf16[128,2,128,128]{3,2,1,0:T(8,128)(2,1)}, u32[]{:S(2)}) copy-start(bf16[128,2,128,128]{3,2,1,0:T(8,128)(2,1)} %exchange.1.source) | copy-start | bytes 25165828

commit v2 on v1

v2 whole, which is shorter than its diff:
```python
import functools

import jax
import jax.numpy as jnp
from jax import lax
from jax.experimental import pallas as pl
from jax.experimental.pallas import tpu as pltpu
from jax.sharding import PartitionSpec as P

MESH = pl.DeviceIdType.MESH
REQ = 4
PARTS = 4
SPAN = 12.5
LEVELS = 32767.0
COND_MID = 0.55
COND_STEPS = 32766.0 / 0.45


def lists(quadrupoles, per_group, groups):
    me = lax.axis_index("elec")
    ids = jnp.arange(per_group * groups, dtype=jnp.int32)
    owner = ids // per_group
    away = (owner - me) % groups
    named = jnp.any(quadrupoles[:, 2:4].reshape(-1)[:, None] == ids[None, :], axis=0)
    before = (owner[:, None] == owner[None, :]) & (ids[None, :] < ids[:, None])
    rank = jnp.sum((before & named[None, :]).astype(jnp.int32), axis=1)
    other = (away - 1) * REQ + jnp.minimum(rank, REQ - 1)
    slot = jnp.where(away == 0, ids - me * per_group, other)
    index = jnp.sum(jnp.where(quadrupoles[:, :, None] == ids, slot, 0), axis=-1)
    steps = jnp.arange(groups, dtype=jnp.int32)[:, None, None]
    lanes = jnp.arange(128, dtype=jnp.int32)[None, :, None]
    hit = named & (away == steps) & (rank == lanes)
    asked = jnp.sum(jnp.where(hit, ids % per_group, 0), axis=-1)
    return index.astype(jnp.int32), jnp.broadcast_to(asked[:, None, :], (groups, 8, 128))


def minus(first, second):
    return first.astype(jnp.float32) - second.astype(jnp.float32)


def decode(code):
    root = code.astype(jnp.int32).astype(jnp.float32) * (SPAN**0.125 / LEVELS)
    square = root * root
    fourth = square * square
    return (root * jnp.abs(root)) * square * fourth


def encode(step):
    level = jnp.exp2(jnp.log2(jnp.abs(step) * (1.0 / SPAN)) * 0.125) * LEVELS
    level = (level + 0.5).astype(jnp.int32)
    return jnp.where(step < 0, -level, level).astype(jnp.int16)


def exchange_kernel(slabs, groups, *refs):
    pot, cond, asked, index, out = refs[:5]
    pot_v, cond_v, stage, enc, cin, field, cond_code, cond_in = refs[5:13]
    asked_in, asked_s, place_v, place_s, own, box = refs[13:19]
    far = refs[19 : 19 + slabs]
    plane_send, plane_recv, fwd_send, cond_send, cond_recv = refs[19 + slabs : 24 + slabs]
    ask_send, ask_recv, far_send, far_recv, pot_sem, local = refs[24 + slabs :]

    count, depth, rows, width = pot.shape
    slots = rows + 1
    some = count // 2
    half = slabs // 2
    x_size = rows * slabs
    tall = x_size + 16
    readings = out.shape[0]
    me = lax.axis_index("slab")
    group = lax.axis_index("elec")
    upper = me // half
    near0 = upper * half
    far0 = (1 - upper) * half
    my_rows = pl.ds(pl.multiple_of(me * rows, rows), rows)

    share = count // PARTS
    loads = [
        pltpu.make_async_copy(pot.at[pl.ds(k * share, share)], pot_v.at[pl.ds(k * share, share)], pot_sem.at[k])
        for k in range(PARTS)
    ]
    cond_load = pltpu.make_async_copy(cond, cond_v, local.at[0])

    barrier = pltpu.get_barrier_semaphore()
    for step in range(1, groups):
        pl.semaphore_signal(barrier, inc=1, device_id={"elec": lax.rem(group + step, groups)}, device_id_type=MESH)
    for step in range(1, slabs):
        pl.semaphore_signal(barrier, inc=1, device_id={"slab": lax.rem(me + step, slabs)}, device_id_type=MESH)
    for copy in loads:
        copy.start()
    cond_load.start()

    blank = jnp.zeros((2, slots, some, width), jnp.int16)
    enc[0] = blank
    enc[depth + 1] = blank

    @pl.when(me == 0)
    def _():
        @pl.loop(1, slabs)
        def _(r):
            cin[r, 0] = blank

    @pl.when(me == slabs - 1)
    def _():
        @pl.loop(0, slabs - 1)
        def _(r):
            cin[r, 3] = blank

    @pl.loop(0, 2 * count)
    def _(k):
        base = (count + k) * tall
        edge = jnp.zeros((8, width), jnp.float32)
        field[pl.ds(pl.multiple_of(base, 8), 8), :] = edge
        field[pl.ds(pl.multiple_of(base + tall - 8, 8), 8), :] = edge

    pl.semaphore_wait(barrier, slabs + groups - 2)

    def ask_copy(step):
        return pltpu.make_async_remote_copy(
            src_ref=asked.at[step],
            dst_ref=asked_in.at[step],
            send_sem=ask_send.at[step],
            recv_sem=ask_recv.at[step],
            device_id={"elec": lax.rem(group + step, groups)},
            device_id_type=MESH,
        )

    for step in range(1, groups):
        ask_copy(step).start()

    def plane_copy(h, slot, d):
        return pltpu.make_async_remote_copy(
            src_ref=enc.at[2 * d + slot, h],
            dst_ref=cin.at[me, slot, h],
            send_sem=plane_send.at[h, slot, d],
            recv_sem=plane_recv.at[h, slot, me],
            device_id={"slab": d},
            device_id_type=MESH,
        )

    def plane_wait(h, slot, r):
        pltpu.make_async_remote_copy(
            src_ref=enc.at[slot, h],
            dst_ref=cin.at[r, slot, h],
            send_sem=plane_send.at[h, slot, r],
            recv_sem=plane_recv.at[h, slot, r],
            device_id={"slab": r},
            device_id_type=MESH,
        ).wait_recv()

    def forward_up(h, r):
        return pltpu.make_async_remote_copy(
            src_ref=cin.at[r, 2, h],
            dst_ref=cin.at[r, 0, h],
            send_sem=fwd_send.at[h, 0, r],
            recv_sem=plane_recv.at[h, 0, r],
            device_id={"slab": lax.rem(me + 1, slabs)},
            device_id_type=MESH,
        )

    def forward_down(h, r):
        return pltpu.make_async_remote_copy(
            src_ref=cin.at[r, 1, h],
            dst_ref=cin.at[r, 3, h],
            send_sem=fwd_send.at[h, 1, r],
            recv_sem=plane_recv.at[h, 3, r],
            device_id={"slab": lax.rem(me + slabs - 1, slabs)},
            device_id_type=MESH,
        )

    ups = (me != slabs - 1) & (me != half - 1)
    downs = (me != 0) & (me != half)

    def cond_copy(step):
        to = lax.rem(me + step, slabs)
        return pltpu.make_async_remote_copy(
            src_ref=cond_code.at[pl.ds(to * 2, 2)],
            dst_ref=cond_in.at[:, my_rows, :],
            send_sem=cond_send.at[step],
            recv_sem=cond_recv.at[step],
            device_id={"slab": to},
            device_id_type=MESH,
        )

    own_cond = pltpu.make_async_copy(cond_code.at[pl.ds(me * 2, 2)], cond_in.at[:, my_rows, :], local.at[1])

    def own_planes(h):
        return pltpu.make_async_copy(enc.at[pl.ds(2 * me, 4), h], cin.at[me, :, h], local.at[4 + h])

    cond_load.wait()

    @pl.loop(0, depth)
    def _(z):
        level = (cond_v[z] - COND_MID) * COND_STEPS
        level = level + jnp.where(level < 0, -0.5, 0.5)
        cond_code[z] = level.astype(jnp.int32).astype(jnp.int16)

    for step in range(1, slabs):
        cond_copy(step).start()
    own_cond.start()

    for step in range(1, groups):
        ask_copy(step).wait_recv()
    asked_copy = pltpu.make_async_copy(asked_in, asked_s, local.at[2])
    asked_copy.start()

    e_row = lax.broadcasted_iota(jnp.int32, (count, width), 0)
    lane = lax.broadcasted_iota(jnp.int32, (count, width), 1)
    hits = jnp.zeros((count, width), jnp.int32)
    for step in range(1, groups):
        wanted = jnp.broadcast_to(asked_in[step, 0:1, :], (count, width))
        hits = hits + jnp.where((wanted == e_row) & (lane < REQ), 1, 0)
    mark = jnp.broadcast_to(jnp.minimum(jnp.sum(hits, axis=1, keepdims=True), 1), (count, width))
    total = jnp.sum(mark, axis=0, keepdims=True)
    before = jnp.sum(jnp.where(e_row < lane, mark, 0), axis=0, keepdims=True)
    here = jnp.sum(jnp.where(e_row == lane, mark, 0), axis=0, keepdims=True)
    place = jnp.where(here > 0, before, total + lane[0:1] - before)
    across = jnp.broadcast_to(place, (count, width))
    down = jnp.sum(jnp.where(e_row == lane, across, 0), axis=1, keepdims=True)
    order = jnp.sum(jnp.where(jnp.broadcast_to(down, (count, width)) == lane, e_row, 0), axis=0, keepdims=True)
    eight = lax.broadcasted_iota(jnp.int32, (8, width), 0)
    place_v[...] = jnp.where(eight == 0, jnp.broadcast_to(place, (8, width)), jnp.broadcast_to(order, (8, width)))
    place_copy = pltpu.make_async_copy(place_v, place_s, local.at[3])
    place_copy.start()
    asked_copy.wait()
    place_copy.wait()
    for copy in loads:
        copy.wait()

    def edge_copies(h, d, act):
        close = d // half == upper

        @pl.when((d > 0) & (close | (d == half)))
        def _():
            act(plane_copy(h, 0, d))

        @pl.when((d < slabs - 1) & (close | (d == half - 1)))
        def _():
            act(plane_copy(h, 3, d))

    facing = jnp.where(upper == 0, half, half - 1)

    @pl.loop(0, 8)
    def _(n):
        h, kind = n // 4, lax.rem(n, 4)
        d0 = jnp.where(kind < 2, far0, near0)
        z0 = 2 * d0 + lax.rem(kind, 2)

        @pl.loop(0, some)
        def _(j):
            e = place_s[1, h * some + j]
            for q in range(half):
                stage[q, pl.ds(j, rows, stride=some), :] = pot_v[e, z0 + 2 * q]

        reached = [jnp.zeros((some, width), jnp.float32)] * half
        for slot in range(slots):
            for q in range(half):
                code = encode(stage[q, pl.ds(max(slot - 1, 0) * some, some), :] - reached[q])
                enc[z0 + 2 * q + 1, h, slot] = code
                reached[q] = reached[q] + decode(code)

        @pl.when(kind < 2)
        def _():
            @pl.loop(0, half)
            def _(q):
                plane_copy(h, 1 + kind, far0 + q).start()

        @pl.when(kind == 3)
        def _():
            edge_copies(h, facing, lambda copy: copy.start())
            own_planes(h).start()

            @pl.loop(0, half)
            def _(q):
                @pl.when(near0 + q != me)
                def _():
                    plane_copy(h, 1, near0 + q).start()
                    plane_copy(h, 2, near0 + q).start()
                    edge_copies(h, near0 + q, lambda copy: copy.start())

    def decode_plane(h, r, slot):
        reached = jnp.zeros((some, width), jnp.float32)
        for k in range(slots):
            reached = reached + decode(cin[r, slot, h, k])
            if k > 0:
                start = (slot * count + h * some) * tall + 8 + r * rows + k - 1
                field[pl.ds(start, some, stride=tall), :] = reached

    row_lane = lax.broadcasted_iota(jnp.int32, (rows, width), 1)

    def gradients(h, b, flat, steep):
        @pl.loop(h * some, (h + 1) * some)
        def _(e):
            def at(slot, shift):
                return field[pl.ds((slot * count + e) * tall + 8 + b * rows + shift, rows), :]

            for i in steep:
                own[b, e, 0, i] = ((at(2 + i, 0) - at(i, 0)) * 0.5).astype(jnp.bfloat16)
            for i in flat:
                here = at(1 + i, 0)
                right = jnp.where(row_lane < width - 1, pltpu.roll(here, width - 1, 1), 0.0)
                left = jnp.where(row_lane > 0, pltpu.roll(here, 1, 1), 0.0)
                own[b, e, 1, i] = ((at(1 + i, 1) - at(1 + i, -1)) * 0.5).astype(jnp.bfloat16)
                own[b, e, 2, i] = ((right - left) * 0.5).astype(jnp.bfloat16)

    def far_copy(k, step):
        return pltpu.make_async_remote_copy(
            src_ref=box.at[k, step - 1],
            dst_ref=far[k].at[pl.ds((groups - 1 - step) * REQ, REQ)],
            send_sem=far_send.at[k, step],
            recv_sem=far_recv.at[k, step],
            device_id={"elec": lax.rem(group + step, groups)},
            device_id_type=MESH,
        )

    def offer(k, b):
        for step in range(1, groups):
            for which in range(REQ):
                chosen = place_s[0, asked_s[groups - step, 0, which]]
                box[k, step - 1, which] = own[b, chosen]
            far_copy(k, step).start()

    def finish(k, b):
        for step in range(1, groups):
            far_copy(k, step).wait_recv()
        cut = pl.ds(pl.multiple_of(b * rows, rows), rows)
        weights = []
        for i in range(2):
            level = cond_in[i, cut, :].astype(jnp.int32).astype(jnp.float32)
            weights.append(-(level * (1.0 / COND_STEPS) + COND_MID))

        @pl.loop(0, readings // 4)
        def _(block):
            for n in range(4):
                m = block * 4 + n
                first, second = place_s[0, index[4 * m]], place_s[0, index[4 * m + 1]]
                third, fourth = index[4 * m + 2], index[4 * m + 3]
                for i in range(2):
                    total = None
                    for way in range(3):
                        source = minus(own[b, first, way, i], own[b, second, way, i])
                        probe = minus(far[k][third, way, i], far[k][fourth, way, i])
                        total = source * probe if total is None else total + source * probe
                    out[m, i, cut, :] = (weights[i] * total).astype(jnp.bfloat16)

    def take_near(h):
        @pl.loop(0, half)
        def _(j):
            r = near0 + j

            @pl.when(r == me)
            def _():
                own_planes(h).wait()

            @pl.when(r != me)
            def _():
                plane_wait(h, 1, r)
                plane_wait(h, 2, r)

                @pl.when(me > 0)
                def _():
                    plane_wait(h, 0, r)

                @pl.when(me < slabs - 1)
                def _():
                    plane_wait(h, 3, r)

            @pl.loop(0, 4)
            def _(slot):
                decode_plane(h, r, slot)

    def take_far(h, slot):
        @pl.loop(0, half)
        def _(j):
            r = far0 + j
            plane_wait(h, slot, r)

            @pl.when(downs if slot == 1 else ups)
            def _():
                (forward_down if slot == 1 else forward_up)(h, r).start()

            decode_plane(h, r, slot)

    def take_edges(h):
        @pl.loop(0, half)
        def _(j):
            r = far0 + j

            @pl.when(me < slabs - 1)
            def _():
                plane_wait(h, 3, r)

            decode_plane(h, r, 3)

            @pl.when(me > 0)
            def _():
                plane_wait(h, 0, r)

            decode_plane(h, r, 0)

    inside = upper * (half + 1)
    beyond = (1 - upper) * (half - 1)
    both = (0, 1)

    def each(start, number, act):
        @pl.loop(0, number)
        def _(j):
            act(start + j)

    take_near(0)
    take_far(0, 1)
    each(inside, half - 1, lambda b: gradients(0, b, both, both))
    for k in range(half - 1):
        offer(k, inside + k)
    take_far(0, 2)
    take_near(1)
    take_edges(0)
    each(beyond, half + 1, lambda b: gradients(0, b, both, both))
    for k in range(half + 1):
        offer(half - 1 + k, beyond + k)
    each(inside, half - 1, lambda b: gradients(1, b, both, both))
    for step in range(1, slabs):
        cond_copy(step).wait_recv()
    own_cond.wait()
    for k in range(half - 1):
        finish(k, inside + k)
    take_far(1, 1)
    each(beyond, half + 1, lambda b: gradients(1, b, (0,), ()))
    take_far(1, 2)
    each(beyond, half + 1, lambda b: gradients(1, b, (1,), ()))
    take_edges(1)
    each(beyond, half + 1, lambda b: gradients(1, b, (), both))
    for k in range(half + 1):
        finish(half - 1 + k, beyond + k)

    @pl.loop(0, slabs)
    def _(d):
        for h in range(2):

            @pl.when(d != me)
            def _(h=h):
                plane_copy(h, 1, d).wait_send()
                plane_copy(h, 2, d).wait_send()
                edge_copies(h, d, lambda copy: copy.wait_send())

            @pl.when((d // half != upper) & ups)
            def _(h=h):
                forward_up(h, d).wait_send()

            @pl.when((d // half != upper) & downs)
            def _(h=h):
                forward_down(h, d).wait_send()

    for step in range(1, slabs):
        cond_copy(step).wait_send()
    for step in range(1, groups):
        ask_copy(step).wait_send()
    for k in range(slabs):
        for step in range(1, groups):
            far_copy(k, step).wait_send()


def exchange(potentials, conductivity, asked, index, slabs, groups):
    count, depth, rows, width = potentials.shape
    readings = index.shape[0]
    x_size = rows * slabs
    anywhere = pl.BlockSpec(memory_space=pl.ANY)
    dma = pltpu.SemaphoreType.DMA
    bf16, f32, i16, i32 = jnp.bfloat16, jnp.float32, jnp.int16, jnp.int32
    asks = (groups - 1) * REQ
    return pl.pallas_call(
        functools.partial(exchange_kernel, slabs, groups),
        out_shape=pltpu.VMEM((readings, 2, x_size, width), bf16),
        in_specs=[anywhere, anywhere, pl.BlockSpec(memory_space=pltpu.VMEM), pl.BlockSpec(memory_space=pltpu.SMEM)],
        out_specs=pl.BlockSpec(memory_space=pltpu.VMEM),
        scratch_shapes=[
            pltpu.VMEM((count, depth, rows, width), f32),
            pltpu.VMEM((depth, rows, width), f32),
            pltpu.VMEM((slabs // 2, rows * count // 2, width), f32),
            pltpu.VMEM((depth + 2, 2, rows + 1, count // 2, width), i16),
            pltpu.VMEM((slabs, 4, 2, rows + 1, count // 2, width), i16),
            pltpu.VMEM((4 * count * (x_size + 16), width), f32),
            pltpu.VMEM((depth, rows, width), i16),
            pltpu.VMEM((2, x_size, width), i16),
            pltpu.VMEM((groups, 8, 128), i32),
            pltpu.SMEM((groups, 8, 128), i32),
            pltpu.VMEM((8, 128), i32),
            pltpu.SMEM((8, 128), i32),
            pltpu.VMEM((slabs, count, 3, 2, rows, width), bf16),
            pltpu.VMEM((slabs, groups - 1, REQ, 3, 2, rows, width), bf16),
        ]
        + [pltpu.VMEM((asks, 3, 2, rows, width), bf16)] * slabs
        + [
            dma((2, 4, slabs)),
            dma((2, 4, slabs)),
            dma((2, 2, slabs)),
            dma((slabs,)),
            dma((slabs,)),
            dma((groups,)),
            dma((groups,)),
            dma((slabs, groups)),
            dma((slabs, groups)),
            dma((PARTS,)),
            dma((6,)),
        ],
        compiler_params=pltpu.CompilerParams(
            collective_id=0, has_side_effects=True, vmem_limit_bytes=50 * 1024 * 1024
        ),
        name="exchange",
    )(potentials, conductivity, asked, index.reshape(-1))


def deliver_kernel(source, target, done):
    share = source.shape[0] // PARTS
    copies = [
        pltpu.make_async_copy(source.at[pl.ds(k * share, share)], target.at[pl.ds(k * share, share)], done.at[k])
        for k in range(PARTS)
    ]
    for copy in copies:
        copy.start()
    for copy in copies:
        copy.wait()


def deliver(rows):
    return pl.pallas_call(
        deliver_kernel,
        out_shape=jax.ShapeDtypeStruct(rows.shape, rows.dtype),
        in_specs=[pl.BlockSpec(memory_space=pl.ANY)],
        out_specs=pl.BlockSpec(memory_space=pl.ANY),
        scratch_shapes=[pltpu.SemaphoreType.DMA((PARTS,))],
        compiler_params=pltpu.CompilerParams(vmem_limit_bytes=1024 * 1024),
        name="deliver",
    )(rows)


def general(potentials, conductivity, quadrupoles):
    shifted = lax.all_to_all(potentials, "slab", split_axis=1, concat_axis=2, tiled=True)
    cond = lax.all_to_all(conductivity[None], "slab", split_axis=1, concat_axis=2, tiled=True)[0]
    slabs = lax.axis_size("slab")
    ends = slabs - 1
    last = shifted.shape[1] - 1
    below = lax.ppermute(shifted[:, last:], "slab", [(i, i + 1) for i in range(ends)])
    above = lax.ppermute(shifted[:, :1], "slab", [(i + 1, i) for i in range(ends)])
    tall = jnp.concatenate([below, shifted, above], axis=1)
    wide = jnp.pad(shifted, ((0, 0), (0, 0), (1, 1), (1, 1)))
    grads = jnp.stack(
        [
            (tall[:, 2:] - tall[:, :-2]) * 0.5,
            (wide[:, :, 2:, 1:-1] - wide[:, :, :-2, 1:-1]) * 0.5,
            (wide[:, :, 1:-1, 2:] - wide[:, :, 1:-1, :-2]) * 0.5,
        ],
        1,
    ).astype(jnp.bfloat16)
    table = lax.all_gather(grads.reshape(grads.shape[0], 3, -1), "elec", axis=0, tiled=True)
    ids = jnp.arange(table.shape[0], dtype=jnp.int32)
    hot = (quadrupoles[:, :, None] == ids).astype(jnp.bfloat16)
    flat = table.reshape(table.shape[0], -1)
    shape = (quadrupoles.shape[0], 3, -1)
    source = jnp.dot(hot[:, 0] - hot[:, 1], flat, preferred_element_type=jnp.float32).reshape(shape)
    probe = jnp.dot(hot[:, 2] - hot[:, 3], flat, preferred_element_type=jnp.float32).reshape(shape)
    rows = -(cond.reshape(-1)[None] * jnp.sum(source * probe, axis=1))
    return rows.astype(jnp.bfloat16).reshape((quadrupoles.shape[0],) + shifted.shape[1:])


def shards(potentials, conductivity, quadrupoles):
    slabs, groups = lax.axis_size("slab"), lax.axis_size("elec")
    count, depth, rows, width = potentials.shape
    fits = rows == 16 and width == 128 and depth == 2 * slabs and slabs % 4 == 0
    if not fits or count % 32 or 2 * (groups - 1) * REQ > count or count > 128 or quadrupoles.shape[0] % 4:
        return general(potentials, conductivity, quadrupoles)
    index, asked = lists(quadrupoles, count, groups)
    return deliver(exchange(potentials, conductivity, asked, index, slabs, groups))


def solution(mesh):
    in_specs = (P("elec", None, "slab", None), P(None, "slab", None), P("elec", None))
    out_specs = P("elec", "slab", None, None)
    return jax.shard_map(shards, mesh=mesh, in_specs=in_specs, out_specs=out_specs, check_vma=False)
```

time: 136 us -> 123 us (0.904)
  Pallas kernels: 128 us -> 118 us
  local copies, waits for them, and re-layouts: 5.43 us -> 2.36 us
    pallas_call x1, Pallas kernels: 124 us -> 115 us  [exchange(): pl.pallas_call(functools.partial(exchange_kernel, slabs, groups), out_sha...]
    unnamed x4 -> x0, local copies, waits for them, and re-layouts: 4.28 us -> none
where the time goes in v2:
time: 123 us; the launch traced here: 122 us
  Pallas kernels  118 us (96%)
  local copies, waits for them, and re-layouts  2.36 us (2%)
  other arithmetic  1.42 us (1%)
    pallas_call x1, Pallas kernels, exchange(): pl.pallas_call(functools.partial(exchange_kernel, slabs, groups), out_sha...  115 us
    pallas_call x1, Pallas kernels, deliver(): pl.pallas_call(deliver_kernel, out_shape=jax.ShapeDtypeStruct(rows.shape,...  3.37 us

profile of v2, /device:TPU:10, one launch (start us, length us, event | category | flops | bytes accessed | tf_op | source)
XLA Modules:
  0.0 122.3 jit_solution(2446865226272323204)
XLA Ops:
  0.0 0.7 slice.3
  0.7 0.1 copy.7
  0.8 0.1 eq.84
  0.9 0.1 fusion
  1.1 0.2 convert_reduce_fusion
  1.3 0.9 select_reduce_fusion
  2.2 0.1 select_reduce_fusion.1
  2.4 0.6 broadcast_in_dim.18.refs_2_
  3.0 0.1 copy.8
  3.1 0.7 reshape.120.refs_3_
  3.8 115.1 %exchange.1.source = bf16[128,2,128,128]{3,2,1,0:T(8,128)(2,1)S(1)} custom-call(f32[32,16,16,128]{3,2,1,0:T(8,128)} %refs_0_.1, f32[16,16,128]{2,1,0:T(8,128)} %refs_1_.1, s32[4,8,128]{2,1,0:T(8,128)} %broadcast_in_dim.18.refs_2_, s32[512]{0:T(512)} %reshape.120.refs_3_), custom_call_target="tpu_custom_call" | custom-call | tf_op jit(solution)/shard_map/exchange/pallas_call | solution.py:470
  118.9 3.4 %deliver.1 = bf16[128,2,128,128]{3,2,1,0:T(8,128)(2,1)} custom-call(bf16[128,2,128,128]{3,2,1,0:T(8,128)(2,1)S(1)} %exchange.1.source), custom_call_target="tpu_custom_call" | custom-call | tf_op jit(solution)/shard_map/deliver/pallas_call | solution.py:525
  (5 shorter events, 0.1 us)

commit v3 on v2

--- a/solution.py
+++ b/solution.py
@@ -12,6 +12,7 @@
 PARTS = 4
 SPAN = 12.5
 LEVELS = 32767.0
+GROUP = 8
 COND_MID = 0.55
 COND_STEPS = 32766.0 / 0.45
 
@@ -35,7 +36,7 @@
 
 
 def minus(first, second):
-    return first.astype(jnp.float32) - second.astype(jnp.float32)
+    return (first - second).astype(jnp.float32)
 
 
 def decode(code):
@@ -239,6 +240,17 @@
 
     facing = jnp.where(upper == 0, half, half - 1)
 
+    def send_near(h):
+        own_planes(h).start()
+
+        @pl.loop(0, half)
+        def _(q):
+            @pl.when(near0 + q != me)
+            def _():
+                plane_copy(h, 1, near0 + q).start()
+                plane_copy(h, 2, near0 + q).start()
+                edge_copies(h, near0 + q, lambda copy: copy.start())
+
     @pl.loop(0, 8)
     def _(n):
         h, kind = n // 4, lax.rem(n, 4)
@@ -267,15 +279,10 @@
         @pl.when(kind == 3)
         def _():
             edge_copies(h, facing, lambda copy: copy.start())
-            own_planes(h).start()
-
-            @pl.loop(0, half)
-            def _(q):
-                @pl.when(near0 + q != me)
-                def _():
-                    plane_copy(h, 1, near0 + q).start()
-                    plane_copy(h, 2, near0 + q).start()
-                    edge_copies(h, near0 + q, lambda copy: copy.start())
+
+        @pl.when(n == 3)
+        def _():
+            send_near(0)
 
     def decode_plane(h, r, slot):
         reached = jnp.zeros((some, width), jnp.float32)
@@ -288,19 +295,21 @@
     row_lane = lax.broadcasted_iota(jnp.int32, (rows, width), 1)
 
     def gradients(h, b, flat, steep):
-        @pl.loop(h * some, (h + 1) * some)
-        def _(e):
-            def at(slot, shift):
-                return field[pl.ds((slot * count + e) * tall + 8 + b * rows + shift, rows), :]
-
-            for i in steep:
-                own[b, e, 0, i] = ((at(2 + i, 0) - at(i, 0)) * 0.5).astype(jnp.bfloat16)
-            for i in flat:
-                here = at(1 + i, 0)
-                right = jnp.where(row_lane < width - 1, pltpu.roll(here, width - 1, 1), 0.0)
-                left = jnp.where(row_lane > 0, pltpu.roll(here, 1, 1), 0.0)
-                own[b, e, 1, i] = ((at(1 + i, 1) - at(1 + i, -1)) * 0.5).astype(jnp.bfloat16)
-                own[b, e, 2, i] = ((right - left) * 0.5).astype(jnp.bfloat16)
+        @pl.loop(0, some // GROUP)
+        def _(n):
+            for e in [h * some + n * GROUP + g for g in range(GROUP)]:
+
+                def at(slot, shift, e=e):
+                    return field[pl.ds((slot * count + e) * tall + 8 + b * rows + shift, rows), :]
+
+                for i in steep:
+                    own[b, e, 0, i] = ((at(2 + i, 0) - at(i, 0)) * 0.5).astype(jnp.bfloat16)
+                for i in flat:
+                    here = at(1 + i, 0)
+                    right = jnp.where(row_lane < width - 1, pltpu.roll(here, width - 1, 1), 0.0)
+                    left = jnp.where(row_lane > 0, pltpu.roll(here, 1, 1), 0.0)
+                    own[b, e, 1, i] = ((at(1 + i, 1) - at(1 + i, -1)) * 0.5).astype(jnp.bfloat16)
+                    own[b, e, 2, i] = ((right - left) * 0.5).astype(jnp.bfloat16)
 
     def far_copy(k, step):
         return pltpu.make_async_remote_copy(
@@ -323,24 +332,16 @@
         for step in range(1, groups):
             far_copy(k, step).wait_recv()
         cut = pl.ds(pl.multiple_of(b * rows, rows), rows)
-        weights = []
-        for i in range(2):
-            level = cond_in[i, cut, :].astype(jnp.int32).astype(jnp.float32)
-            weights.append(-(level * (1.0 / COND_STEPS) + COND_MID))
-
-        @pl.loop(0, readings // 4)
+        weight = -(cond_in[:, cut, :].astype(jnp.int32).astype(jnp.float32) * (1.0 / COND_STEPS) + COND_MID)
+
+        @pl.loop(0, readings // 8)
         def _(block):
-            for n in range(4):
-                m = block * 4 + n
+            for n in range(8):
+                m = block * 8 + n
                 first, second = place_s[0, index[4 * m]], place_s[0, index[4 * m + 1]]
                 third, fourth = index[4 * m + 2], index[4 * m + 3]
-                for i in range(2):
-                    total = None
-                    for way in range(3):
-                        source = minus(own[b, first, way, i], own[b, second, way, i])
-                        probe = minus(far[k][third, way, i], far[k][fourth, way, i])
-                        total = source * probe if total is None else total + source * probe
-                    out[m, i, cut, :] = (weights[i] * total).astype(jnp.bfloat16)
+                product = minus(own[b, first], own[b, second]) * minus(far[k][third], far[k][fourth])
+                out[m, :, cut, :] = (weight * (product[0] + product[1] + product[2])).astype(jnp.bfloat16)
 
     def take_near(h):
         @pl.loop(0, half)
@@ -406,26 +407,27 @@
         def _(j):
             act(start + j)
 
+    take_far(0, 1)
     take_near(0)
-    take_far(0, 1)
     each(inside, half - 1, lambda b: gradients(0, b, both, both))
     for k in range(half - 1):
         offer(k, inside + k)
     take_far(0, 2)
-    take_near(1)
+    send_near(1)
     take_edges(0)
     each(beyond, half + 1, lambda b: gradients(0, b, both, both))
     for k in range(half + 1):
         offer(half - 1 + k, beyond + k)
+    take_far(1, 1)
+    take_near(1)
     each(inside, half - 1, lambda b: gradients(1, b, both, both))
+    each(beyond, half + 1, lambda b: gradients(1, b, (0,), ()))
+    take_far(1, 2)
     for step in range(1, slabs):
         cond_copy(step).wait_recv()
     own_cond.wait()
     for k in range(half - 1):
         finish(k, inside + k)
-    take_far(1, 1)
-    each(beyond, half + 1, lambda b: gradients(1, b, (0,), ()))
-    take_far(1, 2)
     each(beyond, half + 1, lambda b: gradients(1, b, (1,), ()))
     take_edges(1)
     each(beyond, half + 1, lambda b: gradients(1, b, (), both))
@@ -566,7 +568,7 @@
     slabs, groups = lax.axis_size("slab"), lax.axis_size("elec")
     count, depth, rows, width = potentials.shape
     fits = rows == 16 and width == 128 and depth == 2 * slabs and slabs % 4 == 0
-    if not fits or count % 32 or 2 * (groups - 1) * REQ > count or count > 128 or quadrupoles.shape[0] % 4:
+    if not fits or count % 32 or 2 * (groups - 1) * REQ > count or count > 128 or quadrupoles.shape[0] % 8:
         return general(potentials, conductivity, quadrupoles)
     index, asked = lists(quadrupoles, count, groups)
     return deliver(exchange(potentials, conductivity, asked, index, slabs, groups))

time: 123 us -> 101 us (0.82)
  Pallas kernels: 118 us -> 97.2 us
    pallas_call x1, Pallas kernels: 115 us -> 93.9 us  [exchange(): pl.pallas_call(functools.partial(exchange_kernel, slabs, groups), out_sha...]
where the time goes in v3:
time: 101 us
  Pallas kernels  97.2 us (96%)
  local copies, waits for them, and re-layouts  2.36 us (2%)
  other arithmetic  1.42 us (1%)
    pallas_call x1, Pallas kernels, exchange(): pl.pallas_call(functools.partial(exchange_kernel, slabs, groups), out_sha...  93.9 us
    pallas_call x1, Pallas kernels, deliver(): pl.pallas_call(deliver_kernel, out_shape=jax.ShapeDtypeStruct(rows.shape,...  3.37 us

profile of v3, /device:TPU:10, one launch (start us, length us, event | category | flops | bytes accessed | tf_op | source)
XLA Modules:
  0.0 101.1 jit_solution(15262643645264255251)
XLA Ops:
  0.0 0.7 slice.3
  0.7 0.1 copy.7
  0.8 0.1 eq.84
  0.9 0.1 fusion
  1.1 0.2 convert_reduce_fusion
  1.3 0.9 select_reduce_fusion
  2.2 0.1 select_reduce_fusion.1
  2.4 0.6 broadcast_in_dim.18.refs_2_
  3.0 0.1 copy.8
  3.1 0.7 reshape.120.refs_3_
  3.8 93.9 %exchange.1.source = bf16[128,2,128,128]{3,2,1,0:T(8,128)(2,1)S(1)} custom-call(f32[32,16,16,128]{3,2,1,0:T(8,128)} %refs_0_.1, f32[16,16,128]{2,1,0:T(8,128)} %refs_1_.1, s32[4,8,128]{2,1,0:T(8,128)} %broadcast_in_dim.18.refs_2_, s32[512]{0:T(512)} %reshape.120.refs_3_), custom_call_target="tpu_custom_call" | custom-call | tf_op jit(solution)/shard_map/exchange/pallas_call | solution.py:472
  97.7 3.4 %deliver.1 = bf16[128,2,128,128]{3,2,1,0:T(8,128)(2,1)} custom-call(bf16[128,2,128,128]{3,2,1,0:T(8,128)(2,1)S(1)} %exchange.1.source), custom_call_target="tpu_custom_call" | custom-call | tf_op jit(solution)/shard_map/deliver/pallas_call | solution.py:527
  (5 shorter events, 0.1 us)

commit v4 on v3

--- a/solution.py
+++ b/solution.py
@@ -17,24 +17,6 @@
 COND_STEPS = 32766.0 / 0.45
 
 
-def lists(quadrupoles, per_group, groups):
-    me = lax.axis_index("elec")
-    ids = jnp.arange(per_group * groups, dtype=jnp.int32)
-    owner = ids // per_group
-    away = (owner - me) % groups
-    named = jnp.any(quadrupoles[:, 2:4].reshape(-1)[:, None] == ids[None, :], axis=0)
-    before = (owner[:, None] == owner[None, :]) & (ids[None, :] < ids[:, None])
-    rank = jnp.sum((before & named[None, :]).astype(jnp.int32), axis=1)
-    other = (away - 1) * REQ + jnp.minimum(rank, REQ - 1)
-    slot = jnp.where(away == 0, ids - me * per_group, other)
-    index = jnp.sum(jnp.where(quadrupoles[:, :, None] == ids, slot, 0), axis=-1)
-    steps = jnp.arange(groups, dtype=jnp.int32)[:, None, None]
-    lanes = jnp.arange(128, dtype=jnp.int32)[None, :, None]
-    hit = named & (away == steps) & (rank == lanes)
-    asked = jnp.sum(jnp.where(hit, ids % per_group, 0), axis=-1)
-    return index.astype(jnp.int32), jnp.broadcast_to(asked[:, None, :], (groups, 8, 128))
-
-
 def minus(first, second):
     return (first - second).astype(jnp.float32)
 
@@ -53,12 +35,12 @@
 
 
 def exchange_kernel(slabs, groups, *refs):
-    pot, cond, asked, index, out = refs[:5]
+    pot, cond, quads, index, out = refs[:5]
     pot_v, cond_v, stage, enc, cin, field, cond_code, cond_in = refs[5:13]
-    asked_in, asked_s, place_v, place_s, own, box = refs[13:19]
-    far = refs[19 : 19 + slabs]
-    plane_send, plane_recv, fwd_send, cond_send, cond_recv = refs[19 + slabs : 24 + slabs]
-    ask_send, ask_recv, far_send, far_recv, pot_sem, local = refs[24 + slabs :]
+    asked_in, asked_s, place_v, place_s, asked, spots, own, box = refs[13:21]
+    far = refs[21 : 21 + slabs]
+    plane_send, plane_recv, fwd_send, cond_send, cond_recv = refs[21 + slabs : 26 + slabs]
+    ask_send, ask_recv, far_send, far_recv, pot_sem, local = refs[26 + slabs :]
 
     count, depth, rows, width = pot.shape
     slots = rows + 1
@@ -112,6 +94,28 @@
         edge = jnp.zeros((8, width), jnp.float32)
         field[pl.ds(pl.multiple_of(base, 8), 8), :] = edge
         field[pl.ds(pl.multiple_of(base + tall - 8, 8), 8), :] = edge
+
+    lane = lax.broadcasted_iota(jnp.int32, (width, width), 1)
+    down_id = lax.broadcasted_iota(jnp.int32, (width, width), 0)
+
+    def turned(flat):
+        return jnp.broadcast_to(jnp.sum(jnp.where(down_id == lane, flat, 0), axis=1, keepdims=True), (width, width))
+
+    ids = lax.broadcasted_iota(jnp.int32, (readings, width), 1)
+    third, fourth = (jnp.broadcast_to(quads[:, c : c + 1], (readings, width)) for c in (2, 3))
+    named = jnp.sum(jnp.where((third == ids) | (fourth == ids), 1, 0), axis=0, keepdims=True)
+    named = turned(jnp.broadcast_to(jnp.minimum(named, 1), (width, width)))
+    earlier = (lane // count == down_id // count) & (down_id < lane)
+    rank = jnp.sum(jnp.where(earlier, named, 0), axis=0, keepdims=True)
+    across = lane[0:1]
+    away = lax.rem(across // count - group + groups, groups)
+    spot = jnp.where(away == 0, 0, (away - 1) * REQ + jnp.minimum(rank, REQ - 1))
+    rank_down = turned(jnp.broadcast_to(rank, (width, width)))
+    away_down = lax.rem(down_id // count - group + groups, groups)
+    for step in range(1, groups):
+        hit = (named > 0) & (away_down == step) & (rank_down == lane)
+        chosen = jnp.sum(jnp.where(hit, lax.rem(down_id, count), 0), axis=0, keepdims=True)
+        asked[step] = jnp.broadcast_to(chosen, (8, width))
 
     pl.semaphore_wait(barrier, slabs + groups - 2)
 
@@ -219,7 +223,8 @@
     down = jnp.sum(jnp.where(e_row == lane, across, 0), axis=1, keepdims=True)
     order = jnp.sum(jnp.where(jnp.broadcast_to(down, (count, width)) == lane, e_row, 0), axis=0, keepdims=True)
     eight = lax.broadcasted_iota(jnp.int32, (8, width), 0)
-    place_v[...] = jnp.where(eight == 0, jnp.broadcast_to(place, (8, width)), jnp.broadcast_to(order, (8, width)))
+    table = jnp.where(eight == 0, jnp.broadcast_to(place, (8, width)), jnp.broadcast_to(order, (8, width)))
+    place_v[...] = jnp.where(eight == 2, jnp.broadcast_to(spot, (8, width)), table)
     place_copy = pltpu.make_async_copy(place_v, place_s, local.at[3])
     place_copy.start()
     asked_copy.wait()
@@ -283,6 +288,14 @@
         @pl.when(n == 3)
         def _():
             send_near(0)
+
+    @pl.loop(0, readings // 4)
+    def _(block):
+        for n in range(4):
+            m = block * 4 + n
+            for c in range(2):
+                spots[4 * m + c] = place_s[0, lax.rem(index[4 * m + c], count)]
+                spots[4 * m + 2 + c] = place_s[2, index[4 * m + 2 + c]]
 
     def decode_plane(h, r, slot):
         reached = jnp.zeros((some, width), jnp.float32)
@@ -338,8 +351,7 @@
         def _(block):
             for n in range(8):
                 m = block * 8 + n
-                first, second = place_s[0, index[4 * m]], place_s[0, index[4 * m + 1]]
-                third, fourth = index[4 * m + 2], index[4 * m + 3]
+                first, second, third, fourth = (spots[4 * m + c] for c in range(4))
                 product = minus(own[b, first], own[b, second]) * minus(far[k][third], far[k][fourth])
                 out[m, :, cut, :] = (weight * (product[0] + product[1] + product[2])).astype(jnp.bfloat16)
 
@@ -461,9 +473,9 @@
             far_copy(k, step).wait_send()
 
 
-def exchange(potentials, conductivity, asked, index, slabs, groups):
+def exchange(potentials, conductivity, quadrupoles, slabs, groups):
     count, depth, rows, width = potentials.shape
-    readings = index.shape[0]
+    readings = quadrupoles.shape[0]
     x_size = rows * slabs
     anywhere = pl.BlockSpec(memory_space=pl.ANY)
     dma = pltpu.SemaphoreType.DMA
@@ -487,6 +499,8 @@
             pltpu.SMEM((groups, 8, 128), i32),
             pltpu.VMEM((8, 128), i32),
             pltpu.SMEM((8, 128), i32),
+            pltpu.VMEM((groups, 8, 128), i32),
+            pltpu.SMEM((4 * readings,), i32),
             pltpu.VMEM((slabs, count, 3, 2, rows, width), bf16),
             pltpu.VMEM((slabs, groups - 1, REQ, 3, 2, rows, width), bf16),
         ]
@@ -508,7 +522,7 @@
             collective_id=0, has_side_effects=True, vmem_limit_bytes=50 * 1024 * 1024
         ),
         name="exchange",
-    )(potentials, conductivity, asked, index.reshape(-1))
+    )(potentials, conductivity, quadrupoles, quadrupoles.reshape(-1))
 
 
 def deliver_kernel(source, target, done):
@@ -568,10 +582,9 @@
     slabs, groups = lax.axis_size("slab"), lax.axis_size("elec")
     count, depth, rows, width = potentials.shape
     fits = rows == 16 and width == 128 and depth == 2 * slabs and slabs % 4 == 0
-    if not fits or count % 32 or 2 * (groups - 1) * REQ > count or count > 128 or quadrupoles.shape[0] % 8:
+    if not fits or count % 32 or 2 * (groups - 1) * REQ > count or count * groups != width or quadrupoles.shape[0] % 8:
         return general(potentials, conductivity, quadrupoles)
-    index, asked = lists(quadrupoles, count, groups)
-    return deliver(exchange(potentials, conductivity, asked, index, slabs, groups))
+    return deliver(exchange(potentials, conductivity, quadrupoles, slabs, groups))
 
 
 def solution(mesh):

time: 101 us -> 98.9 us (0.979)
  other arithmetic: 1.42 us -> 0 us
    reduce_sum x3 -> x0, other arithmetic: 1.25 us -> none  [the longest x1 0.92 us: lists(): index = jnp.sum(jnp.where(quadrupoles[:, :, None] == ids, slot, 0), axis=-1)]
where the time goes in v4:
time: 98.9 us; the launch traced here: 98.7 us
  Pallas kernels  97.2 us (98%)
  local copies, waits for them, and re-layouts  1.49 us (2%)
    pallas_call x1, Pallas kernels, exchange(): pl.pallas_call(functools.partial(exchange_kernel, slabs, groups), out_sha...  93.8 us
    pallas_call x1, Pallas kernels, deliver(): pl.pallas_call(deliver_kernel, out_shape=jax.ShapeDtypeStruct(rows.shape,...  3.37 us

profile of v4, /device:TPU:10, one launch (start us, length us, event | category | flops | bytes accessed | tf_op | source)
XLA Modules:
  0.0 98.7 jit_solution(1544677497018989794)
XLA Ops:
  0.0 0.8 copy.6.refs_2_
  0.8 0.0 copy-start
  0.8 0.7 reshape.3.refs_3_
  1.5 0.0 copy-done
  1.5 93.8 %exchange.1.source = bf16[128,2,128,128]{3,2,1,0:T(8,128)(2,1)S(1)} custom-call(f32[32,16,16,128]{3,2,1,0:T(8,128)} %refs_0_.1, f32[16,16,128]{2,1,0:T(8,128)} %refs_1_.1, s32[128,4]{1,0:T(8,128)} %copy-done, s32[512]{0:T(512)} %reshape.3.refs_3_), custom_call_target="tpu_custom_call" | custom-call | tf_op jit(solution)/shard_map/exchange/pallas_call | solution.py:484
  95.3 3.4 %deliver.1 = bf16[128,2,128,128]{3,2,1,0:T(8,128)(2,1)} custom-call(bf16[128,2,128,128]{3,2,1,0:T(8,128)(2,1)S(1)} %exchange.1.source), custom_call_target="tpu_custom_call" | custom-call | tf_op jit(solution)/shard_map/deliver/pallas_call | solution.py:541
Async XLA Ops:
  0.8 0.7 copy-start

commit v5 on v4

--- a/solution.py
+++ b/solution.py
@@ -254,6 +254,11 @@
             def _():
                 plane_copy(h, 1, near0 + q).start()
                 plane_copy(h, 2, near0 + q).start()
+
+        @pl.loop(0, half)
+        def _(q):
+            @pl.when(near0 + q != me)
+            def _():
                 edge_copies(h, near0 + q, lambda copy: copy.start())
 
     @pl.loop(0, 8)

time: 98.9 us -> 98.2 us (level)
  the two profiles are of different devices: /device:TPU:10 before, /device:TPU:8 now
where the time goes in v5:
time: 98.2 us; the launch traced here: 98.1 us
  Pallas kernels  96.6 us (98%)
  local copies, waits for them, and re-layouts  1.49 us (2%)
    pallas_call x1, Pallas kernels, exchange(): pl.pallas_call(functools.partial(exchange_kernel, slabs, groups), out_sha...  93.2 us
    pallas_call x1, Pallas kernels, deliver(): pl.pallas_call(deliver_kernel, out_shape=jax.ShapeDtypeStruct(rows.shape,...  3.37 us

profile of v5, /device:TPU:8, one launch (start us, length us, event | category | flops | bytes accessed | tf_op | source)
XLA Modules:
  0.0 98.1 jit_solution(3124767888403855071)
XLA Ops:
  0.0 0.8 copy.6.refs_2_
  0.8 0.0 copy-start
  0.8 0.7 reshape.3.refs_3_
  1.5 0.0 copy-done
  1.5 93.2 %exchange.1.source = bf16[128,2,128,128]{3,2,1,0:T(8,128)(2,1)S(1)} custom-call(f32[32,16,16,128]{3,2,1,0:T(8,128)} %refs_0_.1, f32[16,16,128]{2,1,0:T(8,128)} %refs_1_.1, s32[128,4]{1,0:T(8,128)} %copy-done, s32[512]{0:T(512)} %reshape.3.refs_3_), custom_call_target="tpu_custom_call" | custom-call | tf_op jit(solution)/shard_map/exchange/pallas_call | solution.py:489
  94.7 3.4 %deliver.1 = bf16[128,2,128,128]{3,2,1,0:T(8,128)(2,1)} custom-call(bf16[128,2,128,128]{3,2,1,0:T(8,128)(2,1)S(1)} %exchange.1.source), custom_call_target="tpu_custom_call" | custom-call | tf_op jit(solution)/shard_map/deliver/pallas_call | solution.py:546
Async XLA Ops:
  0.8 0.7 copy-start

commit v6 on v5

--- a/solution.py
+++ b/solution.py
@@ -12,7 +12,7 @@
 PARTS = 4
 SPAN = 12.5
 LEVELS = 32767.0
-GROUP = 8
+GROUP = 16
 COND_MID = 0.55
 COND_STEPS = 32766.0 / 0.45
 
@@ -396,7 +396,9 @@
             def _():
                 (forward_down if slot == 1 else forward_up)(h, r).start()
 
-            decode_plane(h, r, slot)
+        @pl.loop(0, half)
+        def _(j):
+            decode_plane(h, far0 + j, slot)
 
     def take_edges(h):
         @pl.loop(0, half)

time: 98.2 us -> 97.8 us (level)
  the two profiles are of different devices: /device:TPU:8 before, /device:TPU:19 now
where the time goes in v6:
time: 97.8 us; the launch traced here: 97.7 us
  Pallas kernels  96.2 us (98%)
  local copies, waits for them, and re-layouts  1.49 us (2%)
    pallas_call x1, Pallas kernels, exchange(): pl.pallas_call(functools.partial(exchange_kernel, slabs, groups), out_sha...  92.8 us
    pallas_call x1, Pallas kernels, deliver(): pl.pallas_call(deliver_kernel, out_shape=jax.ShapeDtypeStruct(rows.shape,...  3.37 us

profile of v6, /device:TPU:19, one launch (start us, length us, event | category | flops | bytes accessed | tf_op | source)
XLA Modules:
  0.0 97.7 jit_solution(4061676950842283938)
XLA Ops:
  0.0 0.8 copy.6.refs_2_
  0.8 0.0 copy-start
  0.8 0.7 reshape.3.refs_3_
  1.5 0.0 copy-done
  1.5 92.8 %exchange.1.source = bf16[128,2,128,128]{3,2,1,0:T(8,128)(2,1)S(1)} custom-call(f32[32,16,16,128]{3,2,1,0:T(8,128)} %refs_0_.1, f32[16,16,128]{2,1,0:T(8,128)} %refs_1_.1, s32[128,4]{1,0:T(8,128)} %copy-done, s32[512]{0:T(512)} %reshape.3.refs_3_), custom_call_target="tpu_custom_call" | custom-call | tf_op jit(solution)/shard_map/exchange/pallas_call | solution.py:491
  94.3 3.4 %deliver.1 = bf16[128,2,128,128]{3,2,1,0:T(8,128)(2,1)} custom-call(bf16[128,2,128,128]{3,2,1,0:T(8,128)(2,1)S(1)} %exchange.1.source), custom_call_target="tpu_custom_call" | custom-call | tf_op jit(solution)/shard_map/deliver/pallas_call | solution.py:548
Async XLA Ops:
  0.8 0.7 copy-start
